TPU v7x, 512 devices: a whole 4x4x16 slice. The times are simulated.
512 devices in a mesh: sub: 8 (over y, z_hi), row: 8 (over z_lo), col: 8 (over x, core).
Axes of the slice: x: 4, y: 4, z: 16 (z_hi: 2, z_lo: 8; z = z_hi * 8 + z_lo), core: 2. Of those that a mesh axis runs over, the one named last changes fastest.
Arguments:
- root_inverse: float32 [8192, 8192], P(('sub', 'row'), 'col')
- panel: float32 [8192, 2048], P(('sub', 'row'), 'col'), may hold values from -0.125 to 0.125
- pattern: int32 [64, 16], P(('sub', 'row'), 'col'), may hold values from 0 to 1, as said below
- diag_inverse: float32 [2048, 2048], P(('sub', 'row'), 'col')
Outputs:
- off_block: float32 [8192, 2048], P(('sub', 'row'), 'col')
- diag_block: float32 [2048, 2048], P(('sub', 'row'), 'col')
Inputs may be any that keep to these rules, and one draw needn't show every extreme that they name: `pattern`: in every tile row, each aligned group of 2 tile columns (those of one index of col) has exactly one tile marked 1.
All inputs are finite; a program needn't handle non-finite values.
Results may differ from a plain program's by a relative error of at most 0.000078.
Values sent between devices are 32-bit elements; how exact they have to be, the bound alone decides.
A program may use at most 64 MiB of HBM per device.

v0:
```python
import jax
import jax.numpy as jnp
from jax import lax
from jax.sharding import PartitionSpec as P

highest = lax.Precision.HIGHEST


def rows_of_inverse(root_inverse):
    return lax.all_gather(root_inverse, "col", axis=1, tiled=True)


def local(root_inverse, panel, pattern, diag_inverse):
    tile_rows = panel.shape[0]
    marked = pattern[0].astype(jnp.float32)
    column_mask = jnp.repeat(marked, tile_rows)
    masked_panel = panel * column_mask[None, :]
    inverse_full = rows_of_inverse(root_inverse)
    accumulated = jnp.dot(
        inverse_full,
        lax.all_gather(masked_panel, ("sub", "row"), axis=0, tiled=True),
        precision=highest,
        preferred_element_type=jnp.float32,
    )
    off_block = -(accumulated * column_mask[None, :])
    panel_full_row = lax.all_gather(masked_panel, "col", axis=1, tiled=True)
    contribution = lax.dot_general(
        panel_full_row,
        off_block,
        (((0,), (0,)), ((), ())),
        precision=highest,
        preferred_element_type=jnp.float32,
    )
    update = lax.psum_scatter(contribution, ("sub", "row"), scatter_dimension=0, tiled=True)
    diag_block = diag_inverse - update
    return (off_block, diag_block)


def solution(mesh):
    in_specs = (
        P(("sub", "row"), "col"),
        P(("sub", "row"), "col"),
        P(("sub", "row"), "col"),
        P(("sub", "row"), "col"),
    )
    out_specs = (P(("sub", "row"), "col"), P(("sub", "row"), "col"))
    return jax.shard_map(local, mesh=mesh, in_specs=in_specs, out_specs=out_specs, check_vma=False)
```

profile of v0, /device:TPU:6, one launch (start us, length us, event | category | flops | bytes accessed | tf_op | source)
XLA Modules:
  0.0 950.2 jit_solution(14879854118065150119)
XLA Ops:
  7.2 0.0 all-gather.6.cloned.1.call-start
  7.2 0.7 all-gather.6.cloned.1.call-update
  7.9 0.0 all-gather.4.cloned.1.call-start
  7.9 0.7 convert_bitcast_fusion
  8.6 0.1 broadcast_bitcast_fusion
  8.7 1.6 broadcast_multiply_fusion
  10.2 0.0 all-gather.4.cloned.1.call-update
  10.3 0.0 all-gather.8.cloned.1.call-start
  10.3 0.7 all-gather.8.cloned.1.call-update
  11.0 0.0 reduce-scatter.2.cloned.1.call-start
  11.1 41.4 %all-gather.6.cloned.1.call-done = f32[128,8192]{1,0:T(8,128)} async-done(((f32[128,1024]{1,0:T(8,128)}), f32[128,8192]{1,0:T(8,128)}) %all-gather.6.cloned.1.call-update) | async-done | bytes 4194320 | tf_op jit(solution)/shard_map/all_gather | solution.py:10
  52.5 162.4 %all-gather.4.cloned.1.call-done = f32[8192,256]{1,0:T(8,128)} async-done(((f32[128,256]{1,0:T(8,128)}), f32[8192,256]{1,0:T(8,128)}) %all-gather.4.cloned.1.call-update) | async-done | bytes 8388624 | tf_op jit(solution)/shard_map/all_gather | solution.py:21
  214.9 16.3 %fusion = f32[256,128]{1,0:T(8,128)S(1)} fusion(f32[8192,256]{1,0:T(8,128)} %all-gather.4.cloned.1.call-done, f32[128,8192]{1,0:T(8,128)} %all-gather.6.cloned.1.call-done, f32[256]{0:T(256)S(1)} %broadcast_bitcast_fusion), kind=kOutput, calls=%fused_computation.1 | convolution fusion | flops 3221291008 | bytes 12715008 | tf_op jit(solution)/shard_map/dot_general | solution.py:19
  231.2 0.0 copy-start
  231.2 11.0 %all-gather.8.cloned.1.call-done = f32[128,2048]{1,0:T(8,128)} async-done(((f32[128,256]{1,0:T(8,128)}), f32[128,2048]{1,0:T(8,128)}) %all-gather.8.cloned.1.call-update) | async-done | bytes 1048592 | tf_op jit(solution)/shard_map/all_gather | solution.py:26
  242.2 4.4 fusion.1
  246.6 0.0 reduce-scatter.2.cloned.1.call-update
  246.7 0.8 copy.6
  247.4 694.9 %reduce-scatter.2.cloned.1.call-done = f32[32,256]{1,0:T(8,128)} async-done(((f32[2048,256]{1,0:T(8,128)}), f32[32,256]{1,0:T(8,128)}) %reduce-scatter.2.cloned.1.call-update) | async-done | bytes 32784 | tf_op jit(solution)/shard_map/reduce_scatter | solution.py:34
  942.3 0.0 copy-done
  942.3 1.4 sub.3
Async XLA Ops:
  7.2 45.3 %all-gather.6.cloned.1.call-start = ((), (), s32[]{:S(2)}) async-start(), calls=%async_computation.2 | async-start | bytes 4718592 | tf_op jit(solution)/shard_map/all_gather | solution.py:10
  7.9 207.0 %all-gather.4.cloned.1.call-start = ((), (), s32[]{:S(2)}) async-start(), calls=%async_computation.1 | async-start | bytes 8519680 | tf_op jit(solution)/shard_map/all_gather | solution.py:21
  10.3 232.0 %all-gather.8.cloned.1.call-start = ((), (), s32[]{:S(2)}) async-start(), calls=%async_computation.3 | async-start | bytes 1179648 | tf_op jit(solution)/shard_map/all_gather | solution.py:26
  11.0 931.3 %reduce-scatter.2.cloned.1.call-start = ((), (), s32[]{:S(2)}) async-start(), calls=%async_computation.4 | async-start | bytes 2129920 | tf_op jit(solution)/shard_map/reduce_scatter | solution.py:34
  231.2 711.1 %copy-start = (f32[32,256]{1,0:T(8,128)S(1)}, f32[32,256]{1,0:T(8,128)}, u32[]{:S(2)}) copy-start(f32[32,256]{1,0:T(8,128)} %param.7) | copy-start | bytes 98308
Sparse Core Ops, SparseCore 0:
  10.1 42.3 all-gather.5
  56.0 158.8 all-gather.3
  217.6 24.5 all-gather.7
  246.8 695.4 reduce-scatter.1
where the time goes:
time: 951 us; the launch traced here: 950 us
  waiting for transfers between devices  911 us (96%)
  matrix products  20.7 us (2%)
  between operations  13.8 us (1%)
    reduce_scatter x1, waiting for transfers between devices, local(): lax.psum_scatter(contribution, ('sub', 'row'), scatter_dimension=0, tiled...  695 us
    all_gather x1, waiting for transfers between devices, local(): lax.all_gather(masked_panel, ('sub', 'row'), axis=0, tiled=True)  162 us
    all_gather x1, waiting for transfers between devices, rows_of_inverse(): return lax.all_gather(root_inverse, 'col', axis=1, tiled=True)  41.4 us
  transfers between devices with their start and end apart: 4, of which 4 were waited for; matrix products, arithmetic and copies ran while one was open for 2% of the time, Pallas kernels for 0%

commit v1 on v0

v1 whole, which is shorter than its diff:
```python
import functools

import jax
import jax.numpy as jnp
from jax import lax
from jax.experimental import pallas as pl
from jax.experimental.pallas import tpu as pltpu
from jax.sharding import PartitionSpec as P

MESH = pl.DeviceIdType.MESH
T = 128
H = 136
f32, bf16 = jnp.float32, jnp.bfloat16


def device(x, y, z, k):
    return (y * 2 + z // 8, lax.rem(z, 8), x * 2 + k)


def slot_of(z):
    return lax.rem(z, 4) * 4 + z // 4


def split(v):
    hi = v.astype(bf16)
    return hi, (v - hi.astype(f32)).astype(bf16)


def dot3(ah, al, bh, bl):
    d = functools.partial(jnp.dot, preferred_element_type=f32)
    return d(ah, bh) + (d(ah, bl) + d(al, bh))


def arrived(ref, sem):
    pltpu.make_async_copy(ref, ref, sem).wait()


def kernel(
    a_ref, panel_ref, pattern_ref, diag_ref, off_ref, out_ref,
    vsend, abuf, vz, vs, vp, sy, op, ob, osend, oy,
    ahi, alo, vhi, vlo, thi, tlo, ohi, olo, ubuf, un, ured, uf,
    ss_a, rs_a, ss_vp, rs_vp, ss_sy, rs_sy, ss_far, ss_near, rs_vz, ss_sib, rs_sib,
    ss_vps, rs_vps, ss_o, rs_o, ss_oy, rs_oy, ss_un, rs_un, ss_uf, rs_uf,
):
    sub, row, col = lax.axis_index("sub"), lax.axis_index("row"), lax.axis_index("col")
    x, k = col // 2, lax.rem(col, 2)
    y, z = sub // 2, lax.rem(sub, 2) * 8 + row
    ky = y // 2
    ry = lax.rem(y, 2)
    sib = device(x, y, z, 1 - k)

    def zdev(d):
        return device(x, y, lax.rem(z + d + 16, 16), k)

    diag = jnp.logical_and(x == y, k == ky)
    bar = pltpu.get_barrier_semaphore()

    def hello(dev):
        pl.semaphore_signal(bar, inc=1, device_id=dev, device_id_type=MESH)

    hello(sib)
    for j in range(1, 4):
        for kk in range(2):
            hello(device(x, lax.rem(y + j, 4), z, kk))
    for d in (4, -4, 8, 1, -1, -2):
        hello(zdev(d))
    for r in range(2):
        for kk in range(2):
            me = jnp.logical_and(x == y, jnp.logical_and(2 * k + r == y, k == kk))

            @pl.when(jnp.logical_not(me))
            def _():
                hello(device(y, 2 * k + r, z, kk))

    p0 = pattern_ref[0, 0].astype(f32)
    p1 = pattern_ref[0, 1].astype(f32)
    vsend[0:T] = panel_ref[:, 0:T] * p0 + panel_ref[:, T:] * p1
    vsend[T:H] = jnp.zeros((8, T), f32) + p1
    pl.semaphore_wait(bar, 17 - diag.astype(jnp.int32))

    sends = []

    def send(src, dst, ss, rs, dev, start=True):
        c = pltpu.make_async_remote_copy(
            src_ref=src, dst_ref=dst, send_sem=ss, recv_sem=rs,
            device_id=dev, device_id_type=MESH,
        )
        if start:
            c.start()
        return c

    def send_or_keep(me, src, dst, ss, rs, dev):
        c = send(src, dst, ss, rs, dev, start=False)

        @pl.when(me)
        def _():
            pltpu.make_async_copy(src, dst, rs).start()

        @pl.when(jnp.logical_not(me))
        def _():
            c.start()

        sends.append((me, c))

    myslot = slot_of(z)
    for i, d in enumerate((8, 4, -4)):
        sends.append((None, send(vsend, vz.at[myslot], ss_far.at[i], rs_vz.at[myslot], zdev(d))))
    for i, d in enumerate((1, -1, 2)):
        sends.append((None, send(vsend, vz.at[myslot], ss_near.at[0, i], rs_vz.at[myslot], zdev(d))))
    sends.append((None, send(vsend, vs.at[myslot], ss_sib.at[myslot], rs_sib.at[myslot], sib)))
    for j in range(4):
        yy = lax.rem(y + j, 4)
        me = jnp.logical_and(j == 0, k == ky)
        rel = jnp.where(k == ky, 0, 1)
        i = ry * 2 + rel
        dev = device(x, yy, z, ky)
        if j == 0:
            send_or_keep(me, vsend.at[pl.ds(T, 8)], sy.at[i], ss_sy.at[j], rs_sy.at[i], dev)
        else:
            sends.append((None, send(vsend.at[pl.ds(T, 8)], sy.at[i], ss_sy.at[j], rs_sy.at[i], dev)))
    for j in (2, 1, 3, 0):
        dev = device(lax.rem(x + j, 4), x, z, ky)
        i, iv = ry * 2 + k, y * 2 + k
        if j == 0:
            send_or_keep(diag, a_ref, abuf.at[i], ss_a.at[j], rs_a.at[i], dev)
            send_or_keep(diag, vsend, vp.at[iv], ss_vp.at[j], rs_vp.at[iv], dev)
        else:
            sends.append((None, send(a_ref, abuf.at[i], ss_a.at[j], rs_a.at[i], dev)))
            sends.append((None, send(vsend, vp.at[iv], ss_vp.at[j], rs_vp.at[iv], dev)))

    def expand(ref, rel, zs):
        v, s = ref[0:T], ref[T : T + 1]
        v1 = v * s
        rows = pl.ds(pl.multiple_of(zs * T, T), T)
        for q, part in enumerate((v - v1, v1)):
            hi, lo = split(part)
            vhi[rel, rows, q * T : (q + 1) * T] = hi
            vlo[rel, rows, q * T : (q + 1) * T] = lo

    expand(vsend, 0, z)
    for i, d in enumerate((4, -4, 8)):
        zs = lax.rem(z + d + 16, 16)
        s = slot_of(zs)
        tile = vz.at[s]
        arrived(tile, rs_vz.at[s])
        for b, e in enumerate((1, -1, 2)):
            sends.append((None, send(tile, tile, ss_near.at[i + 1, b], rs_vz.at[s], zdev(e))))
        sends.append((None, send(tile, vs.at[s], ss_sib.at[s], rs_sib.at[s], sib)))
        expand(tile, 0, zs)

    for d in (-1, 1, -2):

        def near(i, carry, d=d):
            zs = lax.rem(z + d + 16 + 4 * i, 16)
            s = slot_of(zs)
            tile = vz.at[s]
            arrived(tile, rs_vz.at[s])
            send(tile, vs.at[s], ss_sib.at[s], rs_sib.at[s], sib)
            expand(tile, 0, zs)
            return carry

        lax.fori_loop(0, 4, near, 0)

    for i in range(4):
        arrived(vp.at[4 * k + i], rs_vp.at[4 * k + i])
    mine = vp.at[pl.ds(4 * k, 4)]
    sends.append((None, send(mine, mine, ss_vps, rs_vps, sib)))
    other = vp.at[pl.ds(4 * (1 - k), 4)]
    arrived(other, rs_vps)
    for ya in range(4):
        for kk in range(2):
            ref = vp.at[ya * 2 + kk]
            v, s = ref[0:T], ref[T : T + 1]
            v1 = v * s
            for q, part in enumerate((v - v1, v1)):
                hi, lo = split(part.T)
                rows = slice((kk * 2 + q) * T, (kk * 2 + q + 1) * T)
                thi[rows, ya * T : (ya + 1) * T] = hi
                tlo[rows, ya * T : (ya + 1) * T] = lo

    for r in range(2):
        for kk in range(2):
            i = r * 2 + kk
            arrived(abuf.at[i], rs_a.at[i])
            hi, lo = split(abuf[i])
            ahi[r * T : (r + 1) * T, kk * 1024 : (kk + 1) * 1024] = hi
            alo[r * T : (r + 1) * T, kk * 1024 : (kk + 1) * 1024] = lo

    def from_sibling(i, carry):
        zs = lax.rem(z + i, 16)
        s = slot_of(zs)
        arrived(vs.at[s], rs_sib.at[s])
        expand(vs.at[s], 1, zs)
        return carry

    lax.fori_loop(0, 16, from_sibling, 0)

    for r in range(2):
        for rel in range(2):
            arrived(sy.at[r * 2 + rel], rs_sy.at[r * 2 + rel])
    for rel in range(2):
        acc = dot3(ahi[...], alo[...], vhi[rel], vlo[rel])
        for r in range(2):
            i = r * 2 + rel
            s = sy[i, 0:1]
            rows = acc[r * T : (r + 1) * T]
            op[i] = jnp.where(s > 0.5, rows[:, T:], rows[:, :T])
            me = jnp.logical_and(2 * k + r == y, rel == 0)
            dev = device(x, 2 * k + r, z, k if rel == 0 else 1 - k)
            if rel == 0:
                send_or_keep(me, op.at[i], ob.at[y], ss_o.at[i], rs_o.at[y], dev)
            else:
                sends.append((None, send(op.at[i], ob.at[y], ss_o.at[i], rs_o.at[y], dev)))

    for i in range(4):
        arrived(ob.at[i], rs_o.at[i])
    o = -((ob[0] + ob[1]) + (ob[2] + ob[3]))
    osend[0:T] = o
    osend[T:H] = vsend[T:H]
    for j in range(1, 4):
        dev = device(x, lax.rem(y + j, 4), z, k)
        sends.append((None, send(osend, oy.at[y], ss_oy.at[j - 1], rs_oy.at[y], dev)))
    o1 = o * p1
    off_ref[:, 0:T] = o * p0
    off_ref[:, T:] = o1

    def place(ref, ya):
        v, s = ref[0:T], ref[T : T + 1]
        v1 = v * s
        rows = pl.ds(pl.multiple_of(ya * T, T), T)
        for q, part in enumerate((v - v1, v1)):
            hi, lo = split(part)
            ohi[rows, q * T : (q + 1) * T] = hi
            olo[rows, q * T : (q + 1) * T] = lo

    place(osend, y)
    for j in range(1, 4):
        ya = lax.rem(y + j, 4)
        arrived(oy.at[ya], rs_oy.at[ya])
        place(oy.at[ya], ya)

    for zb in range(4):
        rows = slice(zb * T, (zb + 1) * T)
        u = dot3(thi[rows], tlo[rows], ohi[...], olo[...])
        for zl in range(4):
            ubuf[zl, zb] = u[zl * 32 : (zl + 1) * 32]
    zl, zb = lax.rem(z, 4), z // 4
    for i, d in enumerate((1, -1, 2)):
        sends.append((None, send(ubuf.at[lax.rem(zl + d + 4, 4)], un.at[i], ss_un.at[i], rs_un.at[i], zdev(d))))
    for i in range(3):
        arrived(un.at[i], rs_un.at[i])
    ured[...] = (ubuf[zl] + un[0]) + (un[1] + un[2])
    for j in (2, 1, 3):
        sends.append((None, send(
            ured.at[lax.rem(zb + j, 4)], uf.at[j - 1], ss_uf.at[j - 1], rs_uf.at[j - 1], zdev(4 * j),
        )))
    total = ured[zb]
    for j in range(3):
        arrived(uf.at[j], rs_uf.at[j])
        total = total + uf[j]
    out_ref[...] = diag_ref[...] - total

    for me, c in sends:
        if me is None:
            c.wait_send()
        else:
            pl.when(jnp.logical_not(me))(c.wait_send)

    def sent(i, carry):
        for d in (-1, 1, -2):
            s = slot_of(lax.rem(z + d + 16 + 4 * i, 16))
            send(vz.at[s], vs.at[s], ss_sib.at[s], rs_sib.at[s], sib, start=False).wait_send()
        return carry

    lax.fori_loop(0, 4, sent, 0)


def local(root_inverse, panel, pattern, diag_inverse):
    vmem, dma = pltpu.VMEM, pltpu.SemaphoreType.DMA
    return pl.pallas_call(
        kernel,
        out_shape=(
            jax.ShapeDtypeStruct(panel.shape, f32),
            jax.ShapeDtypeStruct(diag_inverse.shape, f32),
        ),
        in_specs=[
            pl.BlockSpec(memory_space=pltpu.VMEM),
            pl.BlockSpec(memory_space=pltpu.VMEM),
            pl.BlockSpec(memory_space=pltpu.SMEM),
            pl.BlockSpec(memory_space=pltpu.VMEM),
        ],
        out_specs=(pl.BlockSpec(memory_space=pltpu.VMEM), pl.BlockSpec(memory_space=pltpu.VMEM)),
        scratch_shapes=[
            vmem((H, T), f32),
            vmem((4, T, 1024), f32),
            vmem((16, H, T), f32),
            vmem((16, H, T), f32),
            vmem((8, H, T), f32),
            vmem((4, 8, T), f32),
            vmem((4, T, T), f32),
            vmem((4, T, T), f32),
            vmem((H, T), f32),
            vmem((4, H, T), f32),
            vmem((2 * T, 2048), bf16),
            vmem((2 * T, 2048), bf16),
            vmem((2, 2048, 2 * T), bf16),
            vmem((2, 2048, 2 * T), bf16),
            vmem((4 * T, 4 * T), bf16),
            vmem((4 * T, 4 * T), bf16),
            vmem((4 * T, 2 * T), bf16),
            vmem((4 * T, 2 * T), bf16),
            vmem((4, 4, 32, 2 * T), f32),
            vmem((3, 4, 32, 2 * T), f32),
            vmem((4, 32, 2 * T), f32),
            vmem((3, 32, 2 * T), f32),
            dma((4,)), dma((4,)),
            dma((4,)), dma((8,)),
            dma((4,)), dma((4,)),
            dma((3,)), dma((4, 3)), dma((16,)),
            dma((16,)), dma((16,)),
            dma, dma,
            dma((4,)), dma((4,)),
            dma((3,)), dma((4,)),
            dma((3,)), dma((3,)),
            dma((3,)), dma((3,)),
        ],
        compiler_params=pltpu.CompilerParams(
            collective_id=0, has_side_effects=True, vmem_limit_bytes=48 << 20
        ),
    )(root_inverse, panel, pattern, diag_inverse)


def solution(mesh):
    spec = P(("sub", "row"), "col")
    return jax.shard_map(
        local, mesh=mesh, in_specs=(spec,) * 4, out_specs=(spec,) * 2, check_vma=False
    )
```

time: 951 us -> 106 us (0.11)
  the two profiles are of different devices: /device:TPU:6 before, /device:TPU:34 now
where the time goes in v1:
time: 106 us
  Pallas kernels  100 us (94%)
  local copies, waits for them, and re-layouts  4.62 us (4%)
    pallas_call x1, Pallas kernels, local(): pl.pallas_call(kernel, out_shape=(jax.ShapeDtypeStruct(panel.shape, f32),...  100 us
    unnamed x10, local copies, waits for them, and re-layouts  4.62 us

profile of v1, /device:TPU:34, one launch (start us, length us, event | category | flops | bytes accessed | tf_op | source)
XLA Modules:
  0.0 105.5 jit_solution(18443421453509769565)
XLA Ops:
  0.6 0.0 copy-start
  0.6 1.0 copy-done
  1.7 0.0 copy-start.1
  1.7 0.9 copy-done.1
  2.6 0.0 copy-start.2
  2.6 0.8 copy-done.2
  3.3 0.0 copy-start.3
  3.3 0.7 copy-done.3
  4.0 100.2 %shard_map.59 = (f32[128,256]{1,0:T(8,128)S(1)}, f32[32,256]{1,0:T(8,128)S(1)}) custom-call(f32[128,1024]{1,0:T(8,128)S(1)} %copy-done, f32[128,256]{1,0:T(8,128)S(1)} %copy-done.1, s32[1,2]{1,0:T(1,128)S(1)} %copy-done.3, f32[32,256]{1,0:T(8,128)S(1)} %copy-done.2), custom_call_target="tpu_custom_call" | custom-call | tf_op jit(solution)/shard_map/pallas_call | solution.py:280
  104.2 0.7 copy.8
  104.9 0.6 copy.9
Async XLA Ops:
  0.6 1.0 copy-start
  1.7 0.9 copy-start.1
  2.6 0.8 copy-start.2
  3.3 0.7 copy-start.3

commit v2 on v1

v2 whole, which is shorter than its diff:
```python
import functools

import jax
import jax.numpy as jnp
from jax import lax
from jax.experimental import pallas as pl
from jax.experimental.pallas import tpu as pltpu
from jax.sharding import PartitionSpec as P

MESH = pl.DeviceIdType.MESH
T = 128
H = 136
f32, bf16 = jnp.float32, jnp.bfloat16


def device(x, y, z, k):
    return (y * 2 + z // 8, lax.rem(z, 8), x * 2 + k)


TREE = (
    (0, (5, -5, 1, -1)),
    (1, (2,)),
    (-1, (-2,)),
    (5, (6, 4, 8)),
    (-5, (-6, -4)),
    (2, ()),
    (-2, ()),
    (4, (3,)),
    (-4, (-3,)),
    (6, (7,)),
    (-6, (-7,)),
    (8, ()),
    (3, ()),
    (-3, ()),
    (7, ()),
    (-7, ()),
)
NEAR, FAR = (1, -1, 2), (8, 4, -4)
STEPS = sorted({c - o for o, to in TREE for c in to} | set(NEAR) | set(FAR))


def split(v):
    hi = v.astype(bf16)
    return hi, (v - hi.astype(f32)).astype(bf16)


def dot3(ah, al, bh, bl):
    d = functools.partial(jnp.dot, preferred_element_type=f32)
    return d(ah, bh) + (d(ah, bl) + d(al, bh))


def arrived(ref, sem):
    pltpu.make_async_copy(ref, ref, sem).wait()


def kernel(
    a_ref, panel_ref, pattern_ref, diag_ref, off_ref, out_ref,
    panel, diag, vsend, abuf, vz, vs, vp, vq, op, ob, osend, oy,
    ahi, alo, vhi, vlo, thi, tlo, ohi, olo, ubuf, un, ured, uf,
    ss_in, ss_a, rs_a, ss_t, rs_p, ss_p, ss_z, rs_z, ss_sib, rs_sib,
    ss_q, rs_q, ss_o, rs_o, ss_oy, rs_oy, ss_un, rs_un, ss_uf, rs_uf,
):
    sub, row, col = lax.axis_index("sub"), lax.axis_index("row"), lax.axis_index("col")
    x, k = col // 2, lax.rem(col, 2)
    y, z = sub // 2, lax.rem(sub, 2) * 8 + row
    ky = y // 2
    ry = lax.rem(y, 2)
    sib = device(x, y, z, 1 - k)

    def zat(d):
        return lax.rem(z + d + 16, 16)

    def zdev(d):
        return device(x, y, zat(d), k)

    on_diagonal = x == y
    keeps = jnp.logical_and(on_diagonal, k == ky)
    bar = pltpu.get_barrier_semaphore()

    def hello(dev):
        pl.semaphore_signal(bar, inc=1, device_id=dev, device_id_type=MESH)

    for d in STEPS:
        hello(zdev(-d))
    for j in range(1, 4):
        hello(device(lax.rem(x + j, 4), y, z, k))
        for kk in range(2):
            hello(device(x, lax.rem(y + j, 4), z, kk))
    hello(sib)

    @pl.when(jnp.logical_not(on_diagonal))
    def _():
        hello(device(y, x, z, k))

    for j in range(4):
        dev = device(lax.rem(x + j, 4), x, z, ky)
        if j == 0:
            pl.when(jnp.logical_not(keeps))(functools.partial(hello, dev))
        else:
            hello(dev)
    here = (
        pltpu.make_async_copy(panel_ref, panel, ss_in.at[0]),
        pltpu.make_async_copy(diag_ref, diag, ss_in.at[1]),
    )
    for c in here:
        c.start()
    here[0].wait()

    p0 = pattern_ref[0, 0].astype(f32)
    p1 = pattern_ref[0, 1].astype(f32)
    vsend[0:T] = panel[:, 0:T] * p0 + panel[:, T:] * p1
    vsend[T:H] = jnp.zeros((8, T), f32) + p1
    here[1].wait()
    pl.semaphore_wait(
        bar, len(STEPS) + 15 - on_diagonal.astype(jnp.int32) - keeps.astype(jnp.int32)
    )

    sends = []

    def send(src, dst, ss, rs, dev, start=True):
        c = pltpu.make_async_remote_copy(
            src_ref=src, dst_ref=dst, send_sem=ss, recv_sem=rs,
            device_id=dev, device_id_type=MESH,
        )
        if start:
            c.start()
            sends.append((None, c))
        return c

    def send_or_keep(me, src, dst, ss, rs, dev):
        c = send(src, dst, ss, rs, dev, start=False)

        @pl.when(me)
        def _():
            pltpu.make_async_copy(src, dst, rs).start()

        @pl.when(jnp.logical_not(me))
        def _():
            c.start()

        sends.append((me, c))

    def halves(ref):
        v, s = ref[0:T], ref[T : T + 1]
        v1 = v * s
        return v - v1, v1

    send_or_keep(on_diagonal, vsend, vp.at[y], ss_t, rs_p.at[y], device(y, x, z, k))
    mine = vp.at[x]
    arrived(mine, rs_p.at[x])

    def expand(ref, rel, zs):
        rows = pl.ds(pl.multiple_of(zs * T, T), T)
        for q, part in enumerate(halves(ref)):
            hi, lo = split(part)
            vhi[rel, rows, q * T : (q + 1) * T] = hi
            vlo[rel, rows, q * T : (q + 1) * T] = lo

    for n, (o, to) in enumerate(TREE):
        zs = zat(-o)
        tile = vz.at[zs] if o else mine
        if o:
            arrived(tile, rs_z.at[zs])
        for c in to:
            send(tile, vz.at[zs], ss_z.at[c + 7], rs_z.at[zs], zdev(c - o))
        send(tile, vs.at[zs], ss_sib.at[zs], rs_sib.at[zs], sib)
        if n == 0:
            for j in (2, 1, 3, 0):
                i = ry * 2 + k
                dev = device(x, lax.rem(y + j, 4), z, ky)
                if j == 0:
                    send_or_keep(k == ky, a_ref, abuf.at[i], ss_a.at[j], rs_a.at[i], dev)
                else:
                    send(a_ref, abuf.at[i], ss_a.at[j], rs_a.at[i], dev)
            for j in (2, 1, 3):
                dev = device(lax.rem(x + j, 4), y, z, k)
                send(mine, vp.at[x], ss_p.at[j - 1], rs_p.at[x], dev)
        expand(tile, 0, zs)

    for j in range(1, 4):
        i = lax.rem(x + j, 4)
        arrived(vp.at[i], rs_p.at[i])
    send(vp, vq, ss_q, rs_q, sib)
    arrived(vq, rs_q)
    for ref, kk in ((vp, k), (vq, 1 - k)):
        for ya in range(4):
            for q, part in enumerate(halves(ref.at[ya])):
                hi, lo = split(part.T)
                thi[kk * 2 + q, :, ya * T : (ya + 1) * T] = hi
                tlo[kk * 2 + q, :, ya * T : (ya + 1) * T] = lo

    for r in range(2):
        for kk in range(2):
            i = r * 2 + kk
            arrived(abuf.at[i], rs_a.at[i])
            hi, lo = split(abuf[i])
            ahi[r * T : (r + 1) * T, kk * 1024 : (kk + 1) * 1024] = hi
            alo[r * T : (r + 1) * T, kk * 1024 : (kk + 1) * 1024] = lo

    for o, _ in TREE:
        zs = zat(-o)
        arrived(vs.at[zs], rs_sib.at[zs])
        expand(vs.at[zs], 1, zs)

    for rel in range(2):
        acc = dot3(ahi[...], alo[...], vhi[rel], vlo[rel])
        for r in range(2):
            i = r * 2 + rel
            s = (vq if rel else vp)[2 * k + r, T : T + 1]
            rows = acc[r * T : (r + 1) * T]
            op[i] = jnp.where(s > 0.5, rows[:, T:], rows[:, :T])
            if rel == 0:
                me = jnp.logical_and(on_diagonal, 2 * k + r == y)
                dev = device(y, 2 * k + r, z, k)
                send_or_keep(me, op.at[i], ob.at[x], ss_o.at[i], rs_o.at[x], dev)
            else:
                dev = device(y, 2 * k + r, z, 1 - k)
                send(op.at[i], ob.at[x], ss_o.at[i], rs_o.at[x], dev)

    for i in range(4):
        arrived(ob.at[i], rs_o.at[i])
    o = -((ob[0] + ob[1]) + (ob[2] + ob[3]))
    osend[0:T] = o
    osend[T:H] = vsend[T:H]
    for j in (2, 1, 3):
        dev = device(x, lax.rem(y + j, 4), z, k)
        send(osend, oy.at[y], ss_oy.at[j - 1], rs_oy.at[y], dev)
    off_ref[:, 0:T] = o * p0
    off_ref[:, T:] = o * p1

    def place(ref, ya):
        rows = pl.ds(pl.multiple_of(ya * T, T), T)
        for q, part in enumerate(halves(ref)):
            hi, lo = split(part)
            ohi[rows, q * T : (q + 1) * T] = hi
            olo[rows, q * T : (q + 1) * T] = lo

    place(osend, y)
    for j in (1, 3, 2):
        ya = lax.rem(y + j, 4)
        arrived(oy.at[ya], rs_oy.at[ya])
        place(oy.at[ya], ya)

    zl, zb = lax.rem(z, 4), z // 4
    for j in (2, 1, 3, 0):
        b = lax.rem(zb + j, 4)
        u = dot3(thi[b], tlo[b], ohi[...], olo[...])
        for i in range(4):
            ubuf[i, b] = u[i * 32 : (i + 1) * 32]
        for i, d in enumerate(NEAR):
            src = ubuf.at[lax.rem(zl + d + 4, 4), b]
            send(src, un.at[i, b], ss_un.at[i, j], rs_un.at[i, b], zdev(d))
    for j in (2, 1, 3, 0):
        b = lax.rem(zb + j, 4)
        for i in range(3):
            arrived(un.at[i, b], rs_un.at[i, b])
        ured[b] = (ubuf[zl, b] + un[0, b]) + (un[1, b] + un[2, b])
        if j:
            send(ured.at[b], uf.at[j - 1], ss_uf.at[j - 1], rs_uf.at[j - 1], zdev(4 * j))
    total = diag[...] - ured[zb]
    for j in (0, 2, 1):
        arrived(uf.at[j], rs_uf.at[j])
        total = total - uf[j]
    out_ref[...] = total

    for me, c in sends:
        if me is None:
            c.wait_send()
        else:
            pl.when(jnp.logical_not(me))(c.wait_send)


def local(root_inverse, panel, pattern, diag_inverse):
    vmem, dma = pltpu.VMEM, pltpu.SemaphoreType.DMA
    return pl.pallas_call(
        kernel,
        out_shape=(
            jax.ShapeDtypeStruct(panel.shape, f32),
            jax.ShapeDtypeStruct(diag_inverse.shape, f32),
        ),
        in_specs=[
            pl.BlockSpec(memory_space=pl.ANY),
            pl.BlockSpec(memory_space=pl.ANY),
            pl.BlockSpec(memory_space=pltpu.SMEM),
            pl.BlockSpec(memory_space=pl.ANY),
        ],
        out_specs=(pl.BlockSpec(memory_space=pltpu.VMEM), pl.BlockSpec(memory_space=pltpu.VMEM)),
        scratch_shapes=[
            vmem((T, 2 * T), f32),
            vmem((32, 2 * T), f32),
            vmem((H, T), f32),
            vmem((4, T, 1024), f32),
            vmem((16, H, T), f32),
            vmem((16, H, T), f32),
            vmem((4, H, T), f32),
            vmem((4, H, T), f32),
            vmem((4, T, T), f32),
            vmem((4, T, T), f32),
            vmem((H, T), f32),
            vmem((4, H, T), f32),
            vmem((2 * T, 2048), bf16),
            vmem((2 * T, 2048), bf16),
            vmem((2, 2048, 2 * T), bf16),
            vmem((2, 2048, 2 * T), bf16),
            vmem((4, T, 4 * T), bf16),
            vmem((4, T, 4 * T), bf16),
            vmem((4 * T, 2 * T), bf16),
            vmem((4 * T, 2 * T), bf16),
            vmem((4, 4, 32, 2 * T), f32),
            vmem((3, 4, 32, 2 * T), f32),
            vmem((4, 32, 2 * T), f32),
            vmem((3, 32, 2 * T), f32),
            dma((2,)),
            dma((4,)), dma((4,)),
            dma, dma((4,)), dma((3,)),
            dma((16,)), dma((16,)),
            dma((16,)), dma((16,)),
            dma, dma,
            dma((4,)), dma((4,)),
            dma((3,)), dma((4,)),
            dma((3, 4)), dma((3, 4)),
            dma((3,)), dma((3,)),
        ],
        compiler_params=pltpu.CompilerParams(
            collective_id=0, has_side_effects=True, vmem_limit_bytes=56 << 20
        ),
    )(root_inverse, panel, pattern, diag_inverse)


def solution(mesh):
    spec = P(("sub", "row"), "col")
    return jax.shard_map(
        local, mesh=mesh, in_specs=(spec,) * 4, out_specs=(spec,) * 2, check_vma=False
    )
```

time: 106 us -> 92 us (0.87)
  the two profiles are of different devices: /device:TPU:34 before, /device:TPU:6 now
where the time goes in v2:
time: 92 us; the launch traced here: 91.8 us
  Pallas kernels  89 us (97%)
  local copies, waits for them, and re-layouts  2.19 us (2%)
    pallas_call x1, Pallas kernels, local(): pl.pallas_call(kernel, out_shape=(jax.ShapeDtypeStruct(panel.shape, f32),...  89 us
    unnamed x4, local copies, waits for them, and re-layouts  2.19 us

profile of v2, /device:TPU:6, one launch (start us, length us, event | category | flops | bytes accessed | tf_op | source)
XLA Modules:
  0.0 91.8 jit_solution(6668167488595676569)
XLA Ops:
  0.6 89.0 %shard_map.59 = (f32[128,256]{1,0:T(8,128)}, f32[32,256]{1,0:T(8,128)}) custom-call(f32[128,1024]{1,0:T(8,128)} %a_ref.1, f32[128,256]{1,0:T(8,128)} %panel_ref.1, s32[1,2]{1,0:T(1,128)} %pattern_ref.1, f32[32,256]{1,0:T(8,128)} %diag_ref.1), custom_call_target="tpu_custom_call" | custom-call | tf_op jit(solution)/shard_map/pallas_call | solution.py:275
  89.6 0.0 copy-start
  89.6 1.6 %copy.8 = f32[128,256]{1,0:T(8,128)} copy(f32[128,256]{1,0:T(8,128)} %get-tuple-element.4) | data formatting | bytes 262144
  91.2 0.0 copy-done
  91.2 0.6 copy.9
Async XLA Ops:
  89.6 1.6 %copy-start = (f32[32,256]{1,0:T(8,128)S(1)}, f32[32,256]{1,0:T(8,128)}, u32[]{:S(2)}) copy-start(f32[32,256]{1,0:T(8,128)} %get-tuple-element.5) | copy-start | bytes 98308

commit v3 on v2

v3 whole, which is shorter than its diff:
```python
import functools

import jax
import jax.numpy as jnp
from jax import lax
from jax.experimental import pallas as pl
from jax.experimental.pallas import tpu as pltpu
from jax.sharding import PartitionSpec as P

MESH = pl.DeviceIdType.MESH
T = 128
H = 136
f32, bf16 = jnp.float32, jnp.bfloat16


def device(x, y, z, k):
    return (y * 2 + z // 8, lax.rem(z, 8), x * 2 + k)


TREE = (
    (0, (5, -5, 1, -1)),
    (1, (2,)),
    (-1, (-2,)),
    (5, (6, 4)),
    (-5, (-6, -4)),
    (2, ()),
    (-2, ()),
    (6, (7,)),
    (-6, (-7,)),
    (4, (3,)),
    (-4, (-3,)),
    (7, (8,)),
    (-7, ()),
    (3, ()),
    (-3, ()),
    (8, ()),
)
PIECES = ((0, 64), (64, 72))
NEAR = (2, 1, -1)
STEPS = sorted({c - o for o, to in TREE for c in to} | set(NEAR))
TURNED = (8, 4, -4)


def split(v):
    hi = v.astype(bf16)
    return hi, (v - hi.astype(f32)).astype(bf16)


def dot3(ah, al, bh, bl):
    d = functools.partial(jnp.dot, preferred_element_type=f32)
    return d(ah, bh) + (d(ah, bl) + d(al, bh))


def arrived(ref, sem):
    pltpu.make_async_copy(ref, ref, sem).wait()


def kernel(
    a_ref, panel_ref, pattern_ref, diag_ref, off_ref, out_ref,
    panel, diag, abuf, vz, vs, vp, vq, sy, op, ob, osend, ohome, oy,
    ahi, alo, vhi, vlo, thi, tlo, ohi, olo, ubuf, un, ured, uf,
    ss_in, ss_a, ss_h, rs_a, ss_t, ss_p, rs_p, ss_z, rs_z, ss_sib, rs_sib, ss_sy, rs_sy,
    ss_q, rs_q, ss_o, rs_o, ss_oh, rs_oh, ss_oy, rs_oy, ss_un, rs_un, ss_uf, rs_uf,
):
    here = (
        pltpu.make_async_copy(panel_ref, panel, ss_in.at[0]),
        pltpu.make_async_copy(diag_ref, diag, ss_in.at[1]),
    )
    for c in here:
        c.start()
    sub, row, col = lax.axis_index("sub"), lax.axis_index("row"), lax.axis_index("col")
    x, k = col // 2, lax.rem(col, 2)
    y, z = sub // 2, lax.rem(sub, 2) * 8 + row
    kx, ky = x // 2, y // 2
    way = 1 - 2 * k
    sib = device(x, y, z, 1 - k)

    def zat(d):
        return lax.rem(z + way * d + 16, 16)

    def zdev(d):
        return device(x, y, zat(d), k)

    def turned(d):
        return device(y, x, zat(d), k)

    on_diagonal = x == y
    bar = pltpu.get_barrier_semaphore()

    def hello(dev):
        pl.semaphore_signal(bar, inc=1, device_id=dev, device_id_type=MESH)

    for d in STEPS:
        hello(zdev(-d))
    for j in range(1, 4):
        for kk in range(2):
            hello(device(lax.rem(x + j, 4), y, z, kk))
            hello(device(x, lax.rem(y + j, 4), z, kk))
    hello(sib)

    @pl.when(jnp.logical_not(on_diagonal))
    def _():
        hello(turned(0))

    here[0].wait()

    p0 = pattern_ref[0, 0].astype(f32)
    p1 = pattern_ref[0, 1].astype(f32)
    vp[y, 0:T] = panel[:, 0:T] * p0 + panel[:, T:] * p1
    vp[y, T:H] = jnp.zeros((8, T), f32) + p1
    pl.semaphore_wait(bar, len(STEPS) + 14 - on_diagonal.astype(jnp.int32))

    sends = []

    def send(src, dst, ss, rs, dev, start=True):
        c = pltpu.make_async_remote_copy(
            src_ref=src, dst_ref=dst, send_sem=ss, recv_sem=rs,
            device_id=dev, device_id_type=MESH,
        )
        if start:
            c.start()
            sends.append((None, c))
        return c

    def send_or_keep(me, src, dst, ss, rs, dev):
        c = send(src, dst, ss, rs, dev, start=False)

        @pl.when(me)
        def _():
            pltpu.make_async_copy(src, dst, rs).start()

        @pl.when(jnp.logical_not(me))
        def _():
            c.start()

        sends.append((me, c))

    def halves(ref):
        v, s = ref[0:T], ref[T : T + 1]
        v1 = v * s
        return v - v1, v1

    v = vp.at[y]
    for n, piece in enumerate(PIECES):
        ds = pl.ds(*piece)
        send_or_keep(
            on_diagonal, vp.at[y, ds], vz.at[z, ds], ss_t.at[n], rs_z.at[n, z], turned(0)
        )
    for j in (2, 1, 3):
        send(v, v, ss_p.at[j - 1], rs_p.at[y], device(x, lax.rem(y + j, 4), z, k))

    def half(i, h):
        return abuf.at[i, pl.ds(h * 64, 64)]

    def send_a():
        i = lax.rem(y, 2) * 2 + k
        for h in (0, 1):
            for j, h in ((1, h), (3, 1 - h), (0, h)):
                src = a_ref.at[pl.ds(h * 64, 64)]
                dev = device(x, lax.rem(y + j, 4), z, ky)
                if j == 0:
                    send_or_keep(k == ky, src, half(i, h), ss_a.at[j, h], rs_a.at[i, h], dev)
                else:
                    send(src, half(i, h), ss_a.at[j, h], rs_a.at[i, h], dev)

    def hand_on_a():
        for r in range(2):
            d = lax.rem(y - 2 * k - r + 4, 4)
            h = jnp.where(d == 1, 0, 1)
            dev = device(x, jnp.where(d == 1, lax.rem(y + 1, 4), lax.rem(y + 3, 4)), z, k)
            for kk in range(2):
                i = r * 2 + kk
                c = send(half(i, h), half(i, h), ss_h.at[i], rs_a.at[i, h], dev, start=False)

                @pl.when(lax.rem(d, 2) == 1)
                def _():
                    arrived(half(i, h), rs_a.at[i, h])
                    c.start()

                sends.append((lax.rem(d, 2) == 0, c))

    def expand(ref, rel, zs):
        rows = pl.ds(pl.multiple_of(zs * T, T), T)
        for q, part in enumerate(halves(ref)):
            hi, lo = split(part)
            vhi[rel, rows, q * T : (q + 1) * T] = hi
            vlo[rel, rows, q * T : (q + 1) * T] = lo

    for o, to in TREE:
        zs = zat(-o)
        tile = vz.at[zs]
        for n, piece in enumerate(PIECES):
            part = vz.at[zs, pl.ds(*piece)]
            arrived(part, rs_z.at[n, zs])
            for c in to:
                send(part, part, ss_z.at[n, c + 7], rs_z.at[n, zs], zdev(c - o))
        send(tile, vs.at[zs], ss_sib.at[zs], rs_sib.at[zs], sib)
        if o == -5:
            hand_on_a()
        if o == 0:
            send_a()
            for j in (2, 1, 3, 0):
                i = lax.rem(x, 2) * 2 + jnp.where(k == kx, 0, 1)
                dev = device(lax.rem(x + j, 4), y, z, kx)
                src = vz.at[z, pl.ds(T, 8)]
                if j == 0:
                    send_or_keep(k == kx, src, sy.at[i], ss_sy.at[j], rs_sy.at[i], dev)
                else:
                    send(src, sy.at[i], ss_sy.at[j], rs_sy.at[i], dev)
        expand(tile, 0, zs)

    for j in range(1, 4):
        i = lax.rem(y + j, 4)
        arrived(vp.at[i], rs_p.at[i])
    send(vp, vq, ss_q, rs_q, sib)
    arrived(vq, rs_q)
    for ref, kk in ((vp, k), (vq, 1 - k)):
        for ya in range(4):
            for q, part in enumerate(halves(ref.at[ya])):
                hi, lo = split(part.T)
                thi[kk * 2 + q, :, ya * T : (ya + 1) * T] = hi
                tlo[kk * 2 + q, :, ya * T : (ya + 1) * T] = lo

    for r in range(2):
        for kk in range(2):
            i = r * 2 + kk
            d = lax.rem(y - 2 * k - r + 4, 4)
            h = jnp.where(d == 1, 0, 1)

            @pl.when(lax.rem(d, 2) == 0)
            def _():
                arrived(half(i, h), rs_a.at[i, h])

            arrived(half(i, 1 - h), rs_a.at[i, 1 - h])
            hi, lo = split(abuf[i])
            ahi[r * T : (r + 1) * T, kk * 1024 : (kk + 1) * 1024] = hi
            alo[r * T : (r + 1) * T, kk * 1024 : (kk + 1) * 1024] = lo

    for o, _ in TREE:
        zs = zat(-o)
        arrived(vs.at[zs], rs_sib.at[zs])
        expand(vs.at[zs], 1, zs)
    for i in range(4):
        arrived(sy.at[i], rs_sy.at[i])

    for rel in range(2):
        acc = dot3(ahi[...], alo[...], vhi[rel], vlo[rel])
        for r in range(2):
            i = r * 2 + rel
            s = sy[i, 0:1]
            rows = acc[r * T : (r + 1) * T]
            op[i] = jnp.where(s > 0.5, rows[:, T:], rows[:, :T])
    for h in range(2):
        ds = pl.ds(h * 64, 64)
        for rel in range(2):
            for r in range(2):
                i = r * 2 + rel
                src, dst = op.at[i, ds], ob.at[x, ds]
                sems = ss_o.at[h, i], rs_o.at[h, x]
                if rel == 0:
                    send_or_keep(2 * k + r == x, src, dst, *sems, device(2 * k + r, y, z, k))
                else:
                    send(src, dst, *sems, device(2 * k + r, y, z, 1 - k))
    osend[T:H] = vz[z, T:H]
    for h, piece in enumerate(PIECES):
        lo = slice(h * 64, h * 64 + 64)
        for i in range(4):
            arrived(ob.at[i, pl.ds(h * 64, 64)], rs_o.at[h, i])
        osend[lo] = -((ob[0, lo] + ob[1, lo]) + (ob[2, lo] + ob[3, lo]))
        for j in (2, 1, 3):
            dev = device(lax.rem(x + j, 4), y, z, k)
            ds = pl.ds(*piece)
            send(osend.at[ds], oy.at[x, ds], ss_oy.at[h, j - 1], rs_oy.at[h, x], dev)
    send_or_keep(on_diagonal, osend.at[pl.ds(0, T)], ohome, ss_oh, rs_oh, turned(0))

    def place(ref, ya):
        rows = pl.ds(pl.multiple_of(ya * T, T), T)
        for q, part in enumerate(halves(ref)):
            hi, lo = split(part)
            ohi[rows, q * T : (q + 1) * T] = hi
            olo[rows, q * T : (q + 1) * T] = lo

    place(osend, x)
    for j in (1, 3, 2):
        xa = lax.rem(x + j, 4)
        for h, piece in enumerate(PIECES):
            arrived(oy.at[xa, pl.ds(*piece)], rs_oy.at[h, xa])
        place(oy.at[xa], xa)

    zl, zb = lax.rem(z, 4), z // 4
    for j in (2, 1, 3, 0):
        b = lax.rem(zb + j, 4)
        u = dot3(thi[b], tlo[b], ohi[...], olo[...])
        for i in range(4):
            ubuf[i, b] = u[i * 32 : (i + 1) * 32]
        for i, d in enumerate(NEAR):
            src = ubuf.at[lax.rem(zl + way * d + 4, 4), b]
            send(src, un.at[i, b], ss_un.at[i, j], rs_un.at[i, b], zdev(d))
    arrived(ohome, rs_oh)
    off_ref[:, 0:T] = ohome[...] * p0
    off_ref[:, T:] = ohome[...] * p1
    for j in (2, 1, 3, 0):
        b = lax.rem(zb + j, 4)
        for i in range(3):
            arrived(un.at[i, b], rs_un.at[i, b])
        ured[b] = (ubuf[zl, b] + un[0, b]) + (un[1, b] + un[2, b])
        dev = device(y, x, lax.rem(z + 4 * j, 16), k)
        if j:
            send(ured.at[b], uf.at[j], ss_uf.at[j], rs_uf.at[j], dev)
        else:
            send_or_keep(on_diagonal, ured.at[b], uf.at[j], ss_uf.at[j], rs_uf.at[j], dev)
    here[1].wait()
    total = diag[...]
    for j in (0, 1, 3, 2):
        arrived(uf.at[j], rs_uf.at[j])
        total = total - uf[j]
    out_ref[...] = total

    for me, c in sends:
        if me is None:
            c.wait_send()
        else:
            pl.when(jnp.logical_not(me))(c.wait_send)


def local(root_inverse, panel, pattern, diag_inverse):
    vmem, dma = pltpu.VMEM, pltpu.SemaphoreType.DMA
    return pl.pallas_call(
        kernel,
        out_shape=(
            jax.ShapeDtypeStruct(panel.shape, f32),
            jax.ShapeDtypeStruct(diag_inverse.shape, f32),
        ),
        in_specs=[
            pl.BlockSpec(memory_space=pl.ANY),
            pl.BlockSpec(memory_space=pl.ANY),
            pl.BlockSpec(memory_space=pltpu.SMEM),
            pl.BlockSpec(memory_space=pl.ANY),
        ],
        out_specs=(pl.BlockSpec(memory_space=pltpu.VMEM), pl.BlockSpec(memory_space=pltpu.VMEM)),
        scratch_shapes=[
            vmem((T, 2 * T), f32),
            vmem((32, 2 * T), f32),
            vmem((4, T, 1024), f32),
            vmem((16, H, T), f32),
            vmem((16, H, T), f32),
            vmem((4, H, T), f32),
            vmem((4, H, T), f32),
            vmem((4, 8, T), f32),
            vmem((4, T, T), f32),
            vmem((4, T, T), f32),
            vmem((H, T), f32),
            vmem((T, T), f32),
            vmem((4, H, T), f32),
            vmem((2 * T, 2048), bf16),
            vmem((2 * T, 2048), bf16),
            vmem((2, 2048, 2 * T), bf16),
            vmem((2, 2048, 2 * T), bf16),
            vmem((4, T, 4 * T), bf16),
            vmem((4, T, 4 * T), bf16),
            vmem((4 * T, 2 * T), bf16),
            vmem((4 * T, 2 * T), bf16),
            vmem((4, 4, 32, 2 * T), f32),
            vmem((3, 4, 32, 2 * T), f32),
            vmem((4, 32, 2 * T), f32),
            vmem((4, 32, 2 * T), f32),
            dma((2,)),
            dma((4, 2)), dma((4,)), dma((4, 2)),
            dma((2,)), dma((3,)), dma((4,)),
            dma((2, 16)), dma((2, 16)),
            dma((16,)), dma((16,)),
            dma((4,)), dma((4,)),
            dma, dma,
            dma((2, 4)), dma((2, 4)),
            dma, dma,
            dma((2, 3)), dma((2, 4)),
            dma((3, 4)), dma((3, 4)),
            dma((4,)), dma((4,)),
        ],
        compiler_params=pltpu.CompilerParams(
            collective_id=0, has_side_effects=True, vmem_limit_bytes=56 << 20
        ),
    )(root_inverse, panel, pattern, diag_inverse)


def solution(mesh):
    spec = P(("sub", "row"), "col")
    return jax.shard_map(
        local, mesh=mesh, in_specs=(spec,) * 4, out_specs=(spec,) * 2, check_vma=False
    )
```

time: 92 us -> 80 us (0.87)
  Pallas kernels: 89 us -> 77 us
    pallas_call x1, Pallas kernels: 89 us -> 77 us  [local(): pl.pallas_call(kernel, out_shape=(jax.ShapeDtypeStruct(panel.shape, f32),...]
where the time goes in v3:
time: 80 us; the launch traced here: 79.8 us
  Pallas kernels  77 us (96%)
  local copies, waits for them, and re-layouts  2.19 us (3%)
    pallas_call x1, Pallas kernels, local(): pl.pallas_call(kernel, out_shape=(jax.ShapeDtypeStruct(panel.shape, f32),...  77 us
    unnamed x4, local copies, waits for them, and re-layouts  2.19 us

profile of v3, /device:TPU:6, one launch (start us, length us, event | category | flops | bytes accessed | tf_op | source)
XLA Modules:
  0.0 79.8 jit_solution(15702622959599185456)
XLA Ops:
  0.6 77.0 %shard_map.59 = (f32[128,256]{1,0:T(8,128)}, f32[32,256]{1,0:T(8,128)}) custom-call(f32[128,1024]{1,0:T(8,128)} %a_ref.1, f32[128,256]{1,0:T(8,128)} %panel_ref.1, s32[1,2]{1,0:T(1,128)} %pattern_ref.1, f32[32,256]{1,0:T(8,128)} %diag_ref.1), custom_call_target="tpu_custom_call" | custom-call | tf_op jit(solution)/shard_map/pallas_call | solution.py:328
  77.6 0.0 copy-start
  77.6 1.6 %copy.8 = f32[128,256]{1,0:T(8,128)} copy(f32[128,256]{1,0:T(8,128)} %get-tuple-element.4) | data formatting | bytes 262144
  79.2 0.0 copy-done
  79.2 0.6 copy.9
Async XLA Ops:
  77.6 1.6 %copy-start = (f32[32,256]{1,0:T(8,128)S(1)}, f32[32,256]{1,0:T(8,128)}, u32[]{:S(2)}) copy-start(f32[32,256]{1,0:T(8,128)} %get-tuple-element.5) | copy-start | bytes 98308

commit v4 on v3

--- a/solution.py
+++ b/solution.py
@@ -37,7 +37,7 @@
 )
 PIECES = ((0, 64), (64, 72))
 NEAR = (2, 1, -1)
-STEPS = sorted({c - o for o, to in TREE for c in to} | set(NEAR))
+STEPS = sorted({c - o for o, to in TREE for c in to})
 TURNED = (8, 4, -4)
 
 
@@ -121,6 +121,14 @@
             c.start()
             sends.append((None, c))
         return c
+
+    def drain():
+        for me, c in sends:
+            if me is None:
+                c.wait_send()
+            else:
+                pl.when(jnp.logical_not(me))(c.wait_send)
+        sends.clear()
 
     def send_or_keep(me, src, dst, ss, rs, dev):
         c = send(src, dst, ss, rs, dev, start=False)
@@ -250,9 +258,8 @@
             s = sy[i, 0:1]
             rows = acc[r * T : (r + 1) * T]
             op[i] = jnp.where(s > 0.5, rows[:, T:], rows[:, :T])
-    for h in range(2):
-        ds = pl.ds(h * 64, 64)
-        for rel in range(2):
+        for h in range(2):
+            ds = pl.ds(h * 64, 64)
             for r in range(2):
                 i = r * 2 + rel
                 src, dst = op.at[i, ds], ob.at[x, ds]
@@ -273,6 +280,8 @@
             send(osend.at[ds], oy.at[x, ds], ss_oy.at[h, j - 1], rs_oy.at[h, x], dev)
     send_or_keep(on_diagonal, osend.at[pl.ds(0, T)], ohome, ss_oh, rs_oh, turned(0))
 
+    drain()
+
     def place(ref, ya):
         rows = pl.ds(pl.multiple_of(ya * T, T), T)
         for q, part in enumerate(halves(ref)):
@@ -296,9 +305,9 @@
         for i, d in enumerate(NEAR):
             src = ubuf.at[lax.rem(zl + way * d + 4, 4), b]
             send(src, un.at[i, b], ss_un.at[i, j], rs_un.at[i, b], zdev(d))
+    drain()
     arrived(ohome, rs_oh)
-    off_ref[:, 0:T] = ohome[...] * p0
-    off_ref[:, T:] = ohome[...] * p1
+    off_ref[...] = ohome[...]
     for j in (2, 1, 3, 0):
         b = lax.rem(zb + j, 4)
         for i in range(3):
@@ -316,19 +325,21 @@
         total = total - uf[j]
     out_ref[...] = total
 
-    for me, c in sends:
-        if me is None:
-            c.wait_send()
-        else:
-            pl.when(jnp.logical_not(me))(c.wait_send)
+    drain()
+
+
+def place_results(o_ref, diag_ref, pattern_ref, off_out, diag_out):
+    off_out[:, 0:T] = o_ref[...] * pattern_ref[0, 0].astype(f32)
+    off_out[:, T:] = o_ref[...] * pattern_ref[0, 1].astype(f32)
+    diag_out[...] = diag_ref[...]
 
 
 def local(root_inverse, panel, pattern, diag_inverse):
     vmem, dma = pltpu.VMEM, pltpu.SemaphoreType.DMA
-    return pl.pallas_call(
+    parts = pl.pallas_call(
         kernel,
         out_shape=(
-            jax.ShapeDtypeStruct(panel.shape, f32),
+            jax.ShapeDtypeStruct((T, T), f32),
             jax.ShapeDtypeStruct(diag_inverse.shape, f32),
         ),
         in_specs=[
@@ -381,6 +392,16 @@
             collective_id=0, has_side_effects=True, vmem_limit_bytes=56 << 20
         ),
     )(root_inverse, panel, pattern, diag_inverse)
+    return pl.pallas_call(
+        place_results,
+        out_shape=tuple(jax.ShapeDtypeStruct(p.shape, f32) for p in (panel, diag_inverse)),
+        in_specs=[
+            pl.BlockSpec(memory_space=pltpu.VMEM),
+            pl.BlockSpec(memory_space=pltpu.VMEM),
+            pl.BlockSpec(memory_space=pltpu.SMEM),
+        ],
+        out_specs=(pl.BlockSpec(memory_space=pltpu.VMEM), pl.BlockSpec(memory_space=pltpu.VMEM)),
+    )(*parts, pattern)
 
 
 def solution(mesh):

time: 80 us -> 79.5 us (level); the launches traced: 79.8 us -> 78.3 us
  local copies, waits for them, and re-layouts: 2.19 us -> 0 us
    unnamed x4 -> x0, local copies, waits for them, and re-layouts: 2.19 us -> none
    pallas_call x1 -> x2, Pallas kernels: 77 us -> 77.7 us  [the longest x1 76.1 us: local(): pl.pallas_call(kernel, out_shape=(jax.ShapeDtypeStruct((T, T), f32), jax....]
where the time goes in v4:
time: 79.5 us; the launch traced here: 78.3 us
  Pallas kernels  77.7 us (98%)
    pallas_call x1, Pallas kernels, local(): pl.pallas_call(kernel, out_shape=(jax.ShapeDtypeStruct((T, T), f32), jax....  76.1 us

profile of v4, /device:TPU:6, one launch (start us, length us, event | category | flops | bytes accessed | tf_op | source)
XLA Modules:
  0.0 78.3 jit_solution(15092564723819217246)
XLA Ops:
  0.6 76.1 %shard_map.59 = (f32[128,128]{1,0:T(8,128)}, f32[32,256]{1,0:T(8,128)}) custom-call(f32[128,1024]{1,0:T(8,128)} %a_ref.1, f32[128,256]{1,0:T(8,128)} %panel_ref.1, s32[1,2]{1,0:T(1,128)} %pattern_ref.3, f32[32,256]{1,0:T(8,128)} %diag_ref.1), custom_call_target="tpu_custom_call" | custom-call | tf_op jit(solution)/shard_map/pallas_call | solution.py:339
  76.8 1.5 %shard_map.60 = (f32[128,256]{1,0:T(8,128)}, f32[32,256]{1,0:T(8,128)}) custom-call(f32[128,128]{1,0:T(8,128)} %get-tuple-element.4.o_ref, f32[32,256]{1,0:T(8,128)} %get-tuple-element.5.diag_ref, s32[1,2]{1,0:T(1,128)} %pattern_ref.3), custom_call_target="tpu_custom_call" | custom-call | tf_op jit(solution)/shard_map/pallas_call | solution.py:395

commit v5 on v4

--- a/solution.py
+++ b/solution.py
@@ -35,6 +35,7 @@
     (-3, ()),
     (8, ()),
 )
+GROUPS = ((0, 1), (1, 3), (3, 5), (5, 7), (7, 11), (11, 15), (15, 16))
 PIECES = ((0, 64), (64, 72))
 NEAR = (2, 1, -1)
 STEPS = sorted({c - o for o, to in TREE for c in to})
@@ -194,14 +195,16 @@
             vhi[rel, rows, q * T : (q + 1) * T] = hi
             vlo[rel, rows, q * T : (q + 1) * T] = lo
 
-    for o, to in TREE:
+    def pass_on(o, to, n):
+        zs = zat(-o)
+        part = vz.at[zs, pl.ds(*PIECES[n])]
+        arrived(part, rs_z.at[n, zs])
+        for c in to:
+            send(part, part, ss_z.at[n, c + 7], rs_z.at[n, zs], zdev(c - o))
+
+    def use(o):
         zs = zat(-o)
         tile = vz.at[zs]
-        for n, piece in enumerate(PIECES):
-            part = vz.at[zs, pl.ds(*piece)]
-            arrived(part, rs_z.at[n, zs])
-            for c in to:
-                send(part, part, ss_z.at[n, c + 7], rs_z.at[n, zs], zdev(c - o))
         send(tile, vs.at[zs], ss_sib.at[zs], rs_sib.at[zs], sib)
         if o == -5:
             hand_on_a()
@@ -216,6 +219,13 @@
                 else:
                     send(src, sy.at[i], ss_sy.at[j], rs_sy.at[i], dev)
         expand(tile, 0, zs)
+
+    for first, last in GROUPS:
+        for n in range(len(PIECES)):
+            for o, to in TREE[first:last]:
+                pass_on(o, to, n)
+        for o, _ in TREE[first:last]:
+            use(o)
 
     for j in range(1, 4):
         i = lax.rem(y + j, 4)

time: 79.5 us -> 81.2 us (1.021)
  the two profiles are of different devices: /device:TPU:6 before, /device:TPU:14 now
where the time goes in v5:
time: 81.2 us; the launch traced here: 81 us
  Pallas kernels  80.4 us (99%)
    pallas_call x1, Pallas kernels, local(): pl.pallas_call(kernel, out_shape=(jax.ShapeDtypeStruct((T, T), f32), jax....  78.9 us

profile of v5, /device:TPU:14, one launch (start us, length us, event | category | flops | bytes accessed | tf_op | source)
XLA Modules:
  0.0 81.0 jit_solution(2906937043362279238)
XLA Ops:
  0.6 78.9 %shard_map.59 = (f32[128,128]{1,0:T(8,128)}, f32[32,256]{1,0:T(8,128)}) custom-call(f32[128,1024]{1,0:T(8,128)} %a_ref.1, f32[128,256]{1,0:T(8,128)} %panel_ref.1, s32[1,2]{1,0:T(1,128)} %pattern_ref.3, f32[32,256]{1,0:T(8,128)} %diag_ref.1), custom_call_target="tpu_custom_call" | custom-call | tf_op jit(solution)/shard_map/pallas_call | solution.py:349
  79.5 1.5 %shard_map.60 = (f32[128,256]{1,0:T(8,128)}, f32[32,256]{1,0:T(8,128)}) custom-call(f32[128,128]{1,0:T(8,128)} %get-tuple-element.4.o_ref, f32[32,256]{1,0:T(8,128)} %get-tuple-element.5.diag_ref, s32[1,2]{1,0:T(1,128)} %pattern_ref.3), custom_call_target="tpu_custom_call" | custom-call | tf_op jit(solution)/shard_map/pallas_call | solution.py:405
